TPU v7x, 32 devices: a whole 2x2x4 slice. The times are simulated.
32 devices in a mesh: wide: 16 (over z, y, core), narrow: 2 (over x).
Axes of the slice: x: 2, y: 2, z: 4, core: 2. Of those that a mesh axis runs over, the one named last changes fastest.
Arguments:
- tokens: bfloat16 [2048, 2, 1024], P('wide', 'narrow'), may hold values from -6 to 6
- document: int32 [2048, 2], P('wide', 'narrow'), may hold values from 0 to 4, as said below
- routing: int32 [2048, 2, 1], P('wide', 'narrow'), may hold values from 0 to 1
- capacity: int32 [2], replicated, may hold values from 40 to 80
- load_before: float32 [2], replicated, may hold values from 0.5 to 1.5
- first_gain: float32 [1024], replicated, may hold values from 0.5 to 1.5
- first_shift: float32 [1024], replicated, may hold values from -1 to 1
- project_in: bfloat16 [1024, 3072], replicated, may hold values from -0.1875 to 0.1875
- project_out: bfloat16 [1024, 1024], replicated, may hold values from -1.5 to 1.5
- second_gain: float32 [1024], replicated, may hold values from 0.5 to 1.5
- second_shift: float32 [1024], replicated, may hold values from -1 to 1
- dense_up: bfloat16 [1024, 4096], replicated, may hold values from -0.1875 to 0.1875
- dense_down: bfloat16 [4096, 1024], replicated, may hold values from -0.09375 to 0.09375
- router: bfloat16 [1024, 2], replicated, may hold values from -0.125 to 0.125
- mixer: bfloat16 [1024, 2], replicated, may hold values from -0.09375 to 0.09375
- mixer_bias: float32 [2], replicated, may hold values from -2 to 2
- expert_up: bfloat16 [1024, 2, 4096], P(None, 'narrow'), may hold values from -0.1875 to 0.1875
- expert_down: bfloat16 [4096, 2, 1024], P(None, 'narrow'), may hold values from -0.1875 to 0.1875
- cotangent: bfloat16 [2048, 2, 1024], P('wide', 'narrow'), may hold values from -6 to 6
Outputs:
- result: bfloat16 [2048, 2, 1024], P('wide', 'narrow')
- input_grad: bfloat16 [2048, 2, 1024], P('wide', 'narrow')
- first_gain_grad: float32 [1024], P('wide')
- first_shift_grad: float32 [1024], P('wide')
- project_in_grad: float32 [1024, 3072], P('wide')
- project_out_grad: float32 [1024, 1024], P('wide')
- second_gain_grad: float32 [1024], P('wide')
- second_shift_grad: float32 [1024], P('wide')
- dense_up_grad: float32 [1024, 4096], P('wide')
- dense_down_grad: float32 [4096, 1024], P('wide')
- router_grad: float32 [1024, 2], P('wide')
- mixer_grad: float32 [1024, 2], P('wide')
- mixer_bias_grad: float32 [2], replicated
- expert_up_grad: float32 [1024, 2, 4096], P('wide', 'narrow')
- expert_down_grad: float32 [4096, 2, 1024], P('wide', 'narrow')
- load_after: float32 [2], replicated
Inputs may be any that keep to these rules, and one draw needn't show every extreme that they name: `document`: along each sequence the numbers never fall.
All inputs are finite; a program needn't handle non-finite values.
Results may differ from a plain program's by a relative error of at most 0.03.
Values may be sent and summed in bfloat16 or wider, within the bound.
No kernel may reach another device: no remote copies, remote signals or barrier semaphores. Data moves between devices by JAX's collectives and lax.ppermute only.
A program may use at most 256 MiB of HBM per device.

v0:
```python
import jax
import jax.numpy as jnp
from jax import lax
from jax.sharding import PartitionSpec as P

HEADS = 16
HEAD_DIM = 64


score_scale = 0.125
norm_eps = 1e-05
momentum = 0.3
masked_score = -1e30


def normalize(inputs, weight_gain, weight_shift):
    average = jnp.mean(inputs, axis=-1, keepdims=True)
    centered = inputs - average
    variance = jnp.mean(centered * centered, axis=-1, keepdims=True)
    return centered * lax.rsqrt(variance + norm_eps) * weight_gain + weight_shift


def smooth(inputs):
    return jax.nn.gelu(inputs, approximate=True)


def block_size(row_total, shard_rows):
    span_rows = shard_rows
    while span_rows * 2 <= 512 and row_total % (span_rows * 2) == 0:
        span_rows = span_rows * 2
    return span_rows


def into_blocks(array, span_rows):
    return array.reshape((array.shape[0] // span_rows, span_rows) + array.shape[1:])


def split_heads(values):
    return values.reshape(values.shape[0], values.shape[1], HEADS, HEAD_DIM)


def allowed_pairs(query_place, query_label, key_place, key_label):
    causal = key_place[None, :] <= query_place[:, None]
    same_label = query_label.T[:, :, None] == key_label.T[:, None, :]
    return (causal[None] & same_label)[:, None]


def pair_terms(
    query_part,
    grad_part,
    norm_part,
    delta_part,
    query_place,
    query_label,
    key_part,
    value_part,
    key_place,
    key_label,
):
    scores = (
        jnp.einsum("qshd,kshd->shqk", query_part, key_part, preferred_element_type=jnp.float32)
        * score_scale
    )
    allowed = allowed_pairs(query_place, query_label, key_place, key_label)
    probs = jnp.where(allowed, jnp.exp(scores - norm_part[..., None]), 0.0)
    grad_probs = jnp.einsum(
        "qshd,kshd->shqk", grad_part, value_part, preferred_element_type=jnp.float32
    )
    grad_scores = (probs * (grad_probs - delta_part[..., None])).astype(jnp.bfloat16)
    return (probs.astype(jnp.bfloat16), grad_scores)


def local(
    tokens,
    document,
    routing,
    capacity,
    load_before,
    first_gain,
    first_shift,
    project_in,
    project_out,
    second_gain,
    second_shift,
    dense_up,
    dense_down,
    router,
    mixer,
    mixer_bias,
    expert_up,
    expert_down,
    cotangent,
):
    shard_rows, seq_count, feature_width = tokens.shape
    row_total = shard_rows * seq_count
    expert_count = capacity.shape[0]
    my_first = lax.axis_index("wide") * shard_rows
    my_last = my_first + shard_rows - 1
    query_place = my_first + jnp.arange(shard_rows, dtype=jnp.int32)
    inputs = tokens.astype(jnp.float32).reshape(row_total, feature_width)
    normed_one = normalize(inputs, first_gain, first_shift).astype(jnp.bfloat16)
    projected = jnp.dot(normed_one, project_in, preferred_element_type=jnp.float32).astype(
        jnp.bfloat16
    )
    query_rows = projected[:, :feature_width].reshape(shard_rows, seq_count, feature_width)
    key_rows = projected[:, feature_width : 2 * feature_width].reshape(
        shard_rows, seq_count, feature_width
    )
    value_rows = projected[:, 2 * feature_width :].reshape(shard_rows, seq_count, feature_width)
    query_heads = split_heads(query_rows)
    start_state = (
        jnp.full((seq_count, HEADS, shard_rows), masked_score, jnp.float32),
        jnp.zeros((seq_count, HEADS, shard_rows), jnp.float32),
        jnp.zeros((shard_rows, seq_count, HEADS, HEAD_DIM), jnp.float32),
    )
    running = start_state
    key_piece = lax.all_gather(key_rows, "wide", axis=0, tiled=True)
    value_piece = lax.all_gather(value_rows, "wide", axis=0, tiled=True)
    label_piece = lax.all_gather(document, "wide", axis=0, tiled=True)
    span_rows = block_size(key_piece.shape[0], shard_rows)
    block_first = span_rows * jnp.arange(key_piece.shape[0] // span_rows, dtype=jnp.int32)

    def advance(running, inputs_block):
        key_block, value_block, label_block, block_start = inputs_block

        def advance_compute(running):
            maxima, totals, accumulated = running
            scores = (
                jnp.einsum(
                    "qshd,kshd->shqk",
                    query_heads,
                    split_heads(key_block),
                    preferred_element_type=jnp.float32,
                )
                * score_scale
            )
            key_place = block_start + jnp.arange(span_rows, dtype=jnp.int32)
            allowed = allowed_pairs(query_place, document, key_place, label_block)
            new_peak = jnp.maximum(
                maxima, jnp.max(jnp.where(allowed, scores, masked_score), axis=-1)
            )
            weights = jnp.where(allowed, jnp.exp(scores - new_peak[..., None]), 0.0)
            factor = jnp.exp(maxima - new_peak)
            totals = totals * factor + jnp.sum(weights, axis=-1)
            update = jnp.einsum(
                "shqk,kshd->qshd",
                weights.astype(jnp.bfloat16),
                split_heads(value_block),
                preferred_element_type=jnp.float32,
            )
            accumulated = accumulated * jnp.transpose(factor, (2, 0, 1))[..., None] + update
            return (new_peak, totals, accumulated)

        return (lax.cond(block_start <= my_last, advance_compute, lambda kept: kept, running), None)

    running, _ = lax.scan(
        advance,
        running,
        (
            into_blocks(key_piece, span_rows),
            into_blocks(value_piece, span_rows),
            into_blocks(label_piece, span_rows),
            block_first,
        ),
    )
    maxima, totals, accumulated = running
    log_total = maxima + jnp.log(totals)
    attended = accumulated / jnp.transpose(totals, (2, 0, 1))[..., None]
    attended_low = attended.astype(jnp.bfloat16).reshape(row_total, feature_width)
    attn_out = jnp.dot(attended_low, project_out, preferred_element_type=jnp.float32)
    hidden = inputs + attn_out
    normed_two = normalize(hidden, second_gain, second_shift).astype(jnp.bfloat16)
    dense_pre = jnp.dot(normed_two, dense_up, preferred_element_type=jnp.float32)
    dense_act = smooth(dense_pre).astype(jnp.bfloat16)
    dense_res = jnp.dot(dense_act, dense_down, preferred_element_type=jnp.float32)
    gates = jax.nn.softmax(jnp.dot(normed_two, router, preferred_element_type=jnp.float32), axis=-1)
    chosen = routing.reshape(row_total)
    onehot = (chosen[:, None] == jnp.arange(expert_count, dtype=jnp.int32)[None, :]).astype(
        jnp.int32
    )
    chosen_gate = jnp.sum(gates * onehot, axis=-1)
    mixing = jax.nn.softmax(
        jnp.dot(normed_two, mixer, preferred_element_type=jnp.float32) + mixer_bias, axis=-1
    )
    earlier = jnp.cumsum(onehot, axis=0) - onehot
    slot_rank = jnp.sum(earlier * onehot, axis=-1)
    limit = jnp.sum(capacity[None, :] * onehot, axis=-1)
    kept_mask = slot_rank < limit
    counts = jnp.sum(onehot * kept_mask[:, None].astype(jnp.int32), axis=0)
    slot_total = row_total * 5 // (4 * expert_count)
    slot_index = chosen * slot_total + slot_rank
    dispatch = (
        (slot_index[None, :] == jnp.arange(expert_count * slot_total, dtype=jnp.int32)[:, None])
        & kept_mask[None, :]
    ).astype(jnp.bfloat16)
    dispatched = (
        jnp.dot(dispatch, normed_two, preferred_element_type=jnp.float32)
        .astype(jnp.bfloat16)
        .reshape(expert_count, 1, slot_total, feature_width)
    )
    received = lax.all_to_all(dispatched, "narrow", split_axis=0, concat_axis=1, tiled=True)
    pre_values = jnp.einsum(
        "ensd,def->ensf", received, expert_up, preferred_element_type=jnp.float32
    )
    activated = smooth(pre_values).astype(jnp.bfloat16)
    produced = jnp.einsum(
        "ensf,fed->ensd", activated, expert_down, preferred_element_type=jnp.float32
    ).astype(jnp.bfloat16)
    returned = lax.all_to_all(produced, "narrow", split_axis=1, concat_axis=0, tiled=True)
    returned, received, expert_pre = (returned, received, pre_values)
    combined = jnp.einsum(
        "rn,rd->nd",
        dispatch,
        returned.reshape(expert_count * slot_total, feature_width),
        preferred_element_type=jnp.float32,
    )
    expert_res = chosen_gate[:, None] * combined
    output = hidden + mixing[:, :1] * dense_res + mixing[:, 1:] * expert_res
    result = output.astype(jnp.bfloat16).reshape(shard_rows, seq_count, feature_width)
    grad_out = cotangent.astype(jnp.float32).reshape(row_total, feature_width)
    grad_dense_res = (mixing[:, :1] * grad_out).astype(jnp.bfloat16)
    grad_expert_res = mixing[:, 1:] * grad_out
    grad_gate = jnp.sum(grad_expert_res * combined, axis=-1)
    grad_mixing = jnp.stack(
        [jnp.sum(grad_out * dense_res, axis=-1), jnp.sum(grad_out * expert_res, axis=-1)], axis=-1
    )
    grad_mix_logits = mixing * (grad_mixing - jnp.sum(mixing * grad_mixing, axis=-1, keepdims=True))
    grad_router_logits = (
        gates * (onehot.astype(jnp.float32) - chosen_gate[:, None]) * grad_gate[:, None]
    )
    token_grad = (chosen_gate[:, None] * grad_expert_res).astype(jnp.bfloat16)
    slot_grad = (
        jnp.dot(dispatch, token_grad, preferred_element_type=jnp.float32)
        .astype(jnp.bfloat16)
        .reshape(expert_count, 1, slot_total, feature_width)
    )
    grad_received = lax.all_to_all(slot_grad, "narrow", split_axis=0, concat_axis=1, tiled=True)
    activated = smooth(expert_pre).astype(jnp.bfloat16)
    expert_down_part = jnp.einsum(
        "ensf,ensd->fed", activated, grad_received, preferred_element_type=jnp.float32
    )
    grad_activated = jnp.einsum(
        "ensd,fed->ensf", grad_received, expert_down, preferred_element_type=jnp.float32
    )
    _, expert_smooth_back = jax.vjp(smooth, expert_pre)
    grad_pre = expert_smooth_back(grad_activated)[0].astype(jnp.bfloat16)
    expert_up_part = jnp.einsum(
        "ensd,ensf->def", received, grad_pre, preferred_element_type=jnp.float32
    )
    grad_sent = jnp.einsum(
        "ensf,def->ensd", grad_pre, expert_up, preferred_element_type=jnp.float32
    ).astype(jnp.bfloat16)
    grad_back = lax.all_to_all(grad_sent, "narrow", split_axis=1, concat_axis=0, tiled=True)
    grad_normed_two = jnp.einsum(
        "rn,rd->nd",
        dispatch,
        grad_back.reshape(expert_count * slot_total, feature_width),
        preferred_element_type=jnp.float32,
    )
    dense_down_part = jnp.einsum(
        "nf,nd->fd", dense_act, grad_dense_res, preferred_element_type=jnp.float32
    )
    grad_dense_act = jnp.einsum(
        "nd,fd->nf", grad_dense_res, dense_down, preferred_element_type=jnp.float32
    )
    _, dense_smooth_back = jax.vjp(smooth, dense_pre)
    grad_dense_pre = dense_smooth_back(grad_dense_act)[0].astype(jnp.bfloat16)
    dense_up_part = jnp.einsum(
        "nd,nf->df", normed_two, grad_dense_pre, preferred_element_type=jnp.float32
    )
    grad_normed_two = grad_normed_two + jnp.einsum(
        "nf,df->nd", grad_dense_pre, dense_up, preferred_element_type=jnp.float32
    )
    normed_wide = normed_two.astype(jnp.float32)
    router_part = jnp.einsum(
        "nd,ne->de", normed_wide, grad_router_logits, precision=lax.Precision.HIGHEST
    )
    grad_normed_two = grad_normed_two + jnp.einsum(
        "ne,de->nd", grad_router_logits, router.astype(jnp.float32), precision=lax.Precision.HIGHEST
    )
    mixer_part = jnp.einsum(
        "nd,nm->dm", normed_wide, grad_mix_logits, precision=lax.Precision.HIGHEST
    )
    mixer_bias_part = jnp.sum(grad_mix_logits, axis=0)
    grad_normed_two = grad_normed_two + jnp.einsum(
        "nm,dm->nd", grad_mix_logits, mixer.astype(jnp.float32), precision=lax.Precision.HIGHEST
    )
    _, second_back = jax.vjp(normalize, hidden, second_gain, second_shift)
    grad_hidden_norm, second_gain_part, second_shift_part = second_back(grad_normed_two)
    grad_hidden = grad_out + grad_hidden_norm
    grad_attn = grad_hidden.astype(jnp.bfloat16)
    project_out_part = jnp.einsum(
        "nd,ne->de", attended_low, grad_attn, preferred_element_type=jnp.float32
    )
    grad_attended = jnp.einsum(
        "ne,de->nd", grad_attn, project_out, preferred_element_type=jnp.float32
    ).astype(jnp.bfloat16)
    grad_rows = grad_attended.reshape(shard_rows, seq_count, feature_width)
    grad_heads = split_heads(grad_rows)
    delta = jnp.transpose(jnp.sum(grad_heads.astype(jnp.float32) * attended, axis=-1), (1, 2, 0))
    zero_heads = jnp.zeros((shard_rows, seq_count, HEADS, HEAD_DIM), jnp.float32)
    key_all, value_all, label_all = (
        lax.all_gather(key_rows, "wide", axis=0, tiled=True),
        lax.all_gather(value_rows, "wide", axis=0, tiled=True),
        lax.all_gather(document, "wide", axis=0, tiled=True),
    )
    scan_span_rows = block_size(key_all.shape[0], shard_rows)
    block_first = scan_span_rows * jnp.arange(key_all.shape[0] // scan_span_rows, dtype=jnp.int32)

    def query_advance(grad_query, inputs_block):
        key_block, value_block, label_block, block_start = inputs_block

        def query_compute(grad_query):
            key_place = block_start + jnp.arange(scan_span_rows, dtype=jnp.int32)
            probs, grad_scores = pair_terms(
                query_heads,
                grad_heads,
                log_total,
                delta,
                query_place,
                document,
                split_heads(key_block),
                split_heads(value_block),
                key_place,
                label_block,
            )
            return (
                grad_query
                + jnp.einsum(
                    "shqk,kshd->qshd",
                    grad_scores,
                    split_heads(key_block),
                    preferred_element_type=jnp.float32,
                )
                * score_scale
            )

        return (
            lax.cond(block_start <= my_last, query_compute, lambda kept: kept, grad_query),
            None,
        )

    grad_query, _ = lax.scan(
        query_advance,
        zero_heads,
        (
            into_blocks(key_all, scan_span_rows),
            into_blocks(value_all, scan_span_rows),
            into_blocks(label_all, scan_span_rows),
            block_first,
        ),
    )
    row_count = shard_rows * lax.axis_size("wide")
    part_rows = block_size(row_count, shard_rows)
    part_first = part_rows * jnp.arange(row_count // part_rows, dtype=jnp.int32)

    def one_block(inputs_block):
        key_block, value_block, label_block, block_start = inputs_block

        def one_compute(unused):
            key_place = block_start + jnp.arange(part_rows, dtype=jnp.int32)
            probs, grad_scores = pair_terms(
                query_heads,
                grad_heads,
                log_total,
                delta,
                query_place,
                document,
                split_heads(key_block),
                split_heads(value_block),
                key_place,
                label_block,
            )
            grad_key = (
                jnp.einsum(
                    "shqk,qshd->kshd", grad_scores, query_heads, preferred_element_type=jnp.float32
                )
                * score_scale
            )
            grad_value = jnp.einsum(
                "shqk,qshd->kshd", probs, grad_heads, preferred_element_type=jnp.float32
            )
            return jnp.concatenate(
                [
                    grad_key.reshape(part_rows, seq_count, feature_width),
                    grad_value.reshape(part_rows, seq_count, feature_width),
                ],
                axis=-1,
            )

        return lax.cond(
            block_start <= my_last,
            one_compute,
            lambda unused: jnp.zeros((part_rows, seq_count, 2 * feature_width), jnp.float32),
            jnp.int32(0),
        )

    terms = lax.map(
        one_block,
        (
            into_blocks(key_all, part_rows),
            into_blocks(value_all, part_rows),
            into_blocks(label_all, part_rows),
            part_first,
        ),
    )
    key_value_grad = lax.psum_scatter(
        terms.reshape(row_count, seq_count, 2 * feature_width).astype(jnp.bfloat16),
        "wide",
        scatter_dimension=0,
        tiled=True,
    ).astype(jnp.float32)
    grad_key = key_value_grad[..., :feature_width]
    grad_value = key_value_grad[..., feature_width:]
    grad_projected = jnp.concatenate(
        [
            grad_query.reshape(row_total, feature_width),
            grad_key.reshape(row_total, feature_width),
            grad_value.reshape(row_total, feature_width),
        ],
        axis=1,
    ).astype(jnp.bfloat16)
    project_in_part = jnp.einsum(
        "nd,ne->de", normed_one, grad_projected, preferred_element_type=jnp.float32
    )
    grad_normed_one = jnp.einsum(
        "ne,de->nd", grad_projected, project_in, preferred_element_type=jnp.float32
    )
    _, first_back = jax.vjp(normalize, inputs, first_gain, first_shift)
    grad_inputs, first_gain_part, first_shift_part = first_back(grad_normed_one)
    input_grad = (
        (grad_hidden + grad_inputs)
        .astype(jnp.bfloat16)
        .reshape(shard_rows, seq_count, feature_width)
    )
    summed = (
        lax.psum_scatter(
            first_gain_part.astype(jnp.bfloat16), "wide", scatter_dimension=0, tiled=True
        ).astype(jnp.float32),
        lax.psum_scatter(
            first_shift_part.astype(jnp.bfloat16), "wide", scatter_dimension=0, tiled=True
        ).astype(jnp.float32),
        lax.psum_scatter(
            project_in_part.astype(jnp.bfloat16), "wide", scatter_dimension=0, tiled=True
        ).astype(jnp.float32),
        lax.psum_scatter(
            project_out_part.astype(jnp.bfloat16), "wide", scatter_dimension=0, tiled=True
        ).astype(jnp.float32),
        lax.psum_scatter(
            second_gain_part.astype(jnp.bfloat16), "wide", scatter_dimension=0, tiled=True
        ).astype(jnp.float32),
        lax.psum_scatter(
            second_shift_part.astype(jnp.bfloat16), "wide", scatter_dimension=0, tiled=True
        ).astype(jnp.float32),
        lax.psum_scatter(
            dense_up_part.astype(jnp.bfloat16), "wide", scatter_dimension=0, tiled=True
        ).astype(jnp.float32),
        lax.psum_scatter(
            dense_down_part.astype(jnp.bfloat16), "wide", scatter_dimension=0, tiled=True
        ).astype(jnp.float32),
        lax.psum_scatter(
            router_part.astype(jnp.bfloat16), "wide", scatter_dimension=0, tiled=True
        ).astype(jnp.float32),
        lax.psum_scatter(
            mixer_part.astype(jnp.bfloat16), "wide", scatter_dimension=0, tiled=True
        ).astype(jnp.float32),
        lax.psum_scatter(
            expert_up_part.astype(jnp.bfloat16), "wide", scatter_dimension=0, tiled=True
        ).astype(jnp.float32),
        lax.psum_scatter(
            expert_down_part.astype(jnp.bfloat16), "wide", scatter_dimension=0, tiled=True
        ).astype(jnp.float32),
    )
    dense_sums = (
        lax.psum(summed[0].astype(jnp.bfloat16), "narrow").astype(jnp.float32),
        lax.psum(summed[1].astype(jnp.bfloat16), "narrow").astype(jnp.float32),
        lax.psum(summed[2].astype(jnp.bfloat16), "narrow").astype(jnp.float32),
        lax.psum(summed[3].astype(jnp.bfloat16), "narrow").astype(jnp.float32),
        lax.psum(summed[4].astype(jnp.bfloat16), "narrow").astype(jnp.float32),
        lax.psum(summed[5].astype(jnp.bfloat16), "narrow").astype(jnp.float32),
        lax.psum(summed[6].astype(jnp.bfloat16), "narrow").astype(jnp.float32),
        lax.psum(summed[7].astype(jnp.bfloat16), "narrow").astype(jnp.float32),
        lax.psum(summed[8].astype(jnp.bfloat16), "narrow").astype(jnp.float32),
        lax.psum(summed[9].astype(jnp.bfloat16), "narrow").astype(jnp.float32),
    )
    count_sum, mixer_bias_sum = lax.psum(
        (counts.astype(jnp.float32), mixer_bias_part), ("wide", "narrow")
    )
    tokens_all = row_total * lax.axis_size("wide") * lax.axis_size("narrow")
    load_after = momentum * load_before + (1.0 - momentum) * (count_sum * expert_count / tokens_all)
    return (
        result,
        input_grad,
        dense_sums[0],
        dense_sums[1],
        dense_sums[2],
        dense_sums[3],
        dense_sums[4],
        dense_sums[5],
        dense_sums[6],
        dense_sums[7],
        dense_sums[8],
        dense_sums[9],
        mixer_bias_sum,
        summed[10],
        summed[11],
        load_after,
    )


def solution(mesh):
    return jax.shard_map(
        local,
        mesh=mesh,
        in_specs=(
            P("wide", "narrow", None),
            P("wide", "narrow"),
            P("wide", "narrow", None),
            P(),
            P(),
            P(),
            P(),
            P(),
            P(),
            P(),
            P(),
            P(),
            P(),
            P(),
            P(),
            P(),
            P(None, "narrow", None),
            P(None, "narrow", None),
            P("wide", "narrow", None),
        ),
        out_specs=(
            P("wide", "narrow", None),
            P("wide", "narrow", None),
            P("wide"),
            P("wide"),
            P("wide", None),
            P("wide", None),
            P("wide"),
            P("wide"),
            P("wide", None),
            P("wide", None),
            P("wide", None),
            P("wide", None),
            P(),
            P("wide", "narrow", None),
            P("wide", "narrow", None),
            P(),
        ),
        check_vma=False,
    )
```

profile of v0, /device:TPU:0, one launch (start us, length us, event | category | flops | bytes accessed | tf_op | source)
XLA Modules:
  0.0 1192.2 jit_solution(16258999006276354425)
XLA Ops:
  16.5 23.2 %all_gather.12 = s32[2048,1]{0,1:T(1,128)S(1)} all-gather(s32[128,1]{0,1:T(1,128)S(1)} %copy-done.29), channel_id=1, replica_groups=mesh['wide'=16,'narrow'=2] {'wide'}, dimensions={0}, use_global_device_ids=true | all-gather | bytes 8704 | tf_op jit(solution)/shard_map/all_gather | solution.py:119
  40.3 28.3 %all-gather.7.cloned.1.call-done = bf16[2048,1024]{1,0:T(8,128)(2,1)} async-done(((bf16[128,1024]{1,0:T(8,128)(2,1)}), bf16[2048,1024]{1,0:T(8,128)(2,1)}) %all-gather.7.cloned.1.call-update) | async-done | bytes 4194320 | tf_op jit(solution)/shard_map/all_gather | solution.py:118
  74.8 45.6 %all-gather.5.cloned.1.call-done = bf16[2048,1024]{1,0:T(8,128)(2,1)} async-done(((bf16[128,1024]{1,0:T(8,128)(2,1)}), bf16[2048,1024]{1,0:T(8,128)(2,1)}) %all-gather.5.cloned.1.call-update) | async-done | bytes 4194320 | tf_op jit(solution)/shard_map/all_gather | solution.py:117
  126.6 10.8 while.40
  186.1 8.1 fusion.73
  195.3 7.0 fusion.92
  219.6 41.9 %while.42 = (s32[]{:T(128)}, bf16[4,512,1,2048]{3,1,0,2:T(8,128)(2,1)}, s32[4]{0:T(128)S(1)}, s32[]{:T(128)}, s32[128,1]{0,1:T(1,128)S(1)}, /*index=5*/s32[4,512...) while((s32[]{:T(128)}, ...), condition=%wide.region_32.33_spmd.clone, body=%wide.region_29.32_spmd.clone.sunk | while | flops 552796800 | bytes 43226424 | solution.py:398
  220.8 13.1 %conditional.11 = (bf16[1,512,1,2048]{1,3,2,0:T(8,128)(2,1)S(1)}) conditional(s32[]{:T(128)} %convert_element_type.435, () %tuple.145, (s32[]{:T(128)}, s32[]{:T(128)}, s32[128,1]{0,1:T(1,128)S(1)}, s32[4,512,1]{1,2,0:T(1,128)S(1)}, s32[]{:T(128)}, /*index=5*/bf16[4,512,1,1024]{1,3,2,0:T(8,128)(2,1)}, bf16[128,1,16,64]{0,3,2,1:T(8,128)(2,1)S(1)}, ...), branch_computations={%region_30.30_spmd, %region_31.31_spmd} | conditional | flops 552796800 | bytes 26447896 | solution.py:391
  264.7 6.6 fusion.65
  271.3 11.2 copy.127
  285.9 7.2 convolution_convert_fusion
  300.1 14.7 %while.41 = (s32[]{:T(128)}, f32[128,1,16,64]{0,3,2,1:T(8,128)S(1)}, s32[4]{0:T(128)S(1)}, s32[]{:T(128)}, bf16[4,512,1,1024]{1,3,2,0:T(8,128)(2,1)}, /*index=5*...) while((s32[]{:T(128)}, ...), condition=%wide.region_28.29_spmd.clone, body=%wide.region_25.28_spmd.clone.sunk | while | flops 409404032 | bytes 17462056 | solution.py:343
  301.3 9.5 conditional.10
  314.8 104.6 %reduce-scatter.28.cloned.1.call-done = bf16[128,2048]{1,0:T(8,128)(2,1)} async-done(((bf16[2048,2048]{1,0:T(8,128)(2,1)}), bf16[128,2048]{1,0:T(8,128)(2,1)}) %reduce-scatter.28.cloned.1.call-update) | async-done | bytes 524304
  425.7 7.5 fusion.66
  435.3 40.4 %all-reduce.4 = (f32[2]{0:T(128)}, f32[2]{0:T(128)S(1)}) all-reduce(f32[2]{0:T(128)S(1)} %get-tuple-element.946, f32[2]{0:T(128)S(1)} %convert_element_type.308), channel_id=1, replica_groups=mesh['wide'=16,'narrow'=2] {'wide','narrow'}, use_global_device_ids=true, to_apply=%region_61.62 | all-reduce | flops 4 | bytes 32 | tf_op jit(solution)/shard_map/psum | solution.py:486
  479.2 57.5 %reduce-scatter.32.cloned.1.call-done = bf16[64,2]{1,0:T(8,128)(2,1)} async-done(((bf16[1024,2]{1,0:T(8,128)(2,1)}), bf16[64,2]{1,0:T(8,128)(2,1)}) %reduce-scatter.32.cloned.1.call-update) | async-done | bytes 272
  537.6 106.8 %reduce-scatter.34.cloned.1.call-done = bf16[64,4096]{1,0:T(8,128)(2,1)} async-done(((bf16[1024,4096]{1,0:T(8,128)(2,1)}), bf16[64,4096]{1,0:T(8,128)(2,1)}) %reduce-scatter.34.cloned.1.call-update) | async-done | bytes 524304
  646.7 62.7 %reduce-scatter.20.cloned.1.call-done = bf16[64,1024]{1,0:T(8,128)(2,1)} async-done(((bf16[1024,1024]{1,0:T(8,128)(2,1)}), bf16[64,1024]{1,0:T(8,128)(2,1)}) %reduce-scatter.20.cloned.1.call-update) | async-done | bytes 131088 | tf_op jit(solution)/shard_map/reduce_scatter | solution.py:446
  709.4 108.2 %reduce-scatter.24.cloned.1.call-done = bf16[256,1024]{1,0:T(8,128)(2,1)} async-done(((bf16[4096,1024]{1,0:T(8,128)(2,1)}), bf16[256,1024]{1,0:T(8,128)(2,1)}) %reduce-scatter.24.cloned.1.call-update) | async-done | bytes 524304 | tf_op jit(solution)/shard_map/reduce_scatter | solution.py:458
  817.7 109.0 %reduce-scatter.22.cloned.1.call-done = bf16[64,4096]{1,0:T(8,128)(2,1)} async-done(((bf16[1024,4096]{1,0:T(8,128)(2,1)}), bf16[64,4096]{1,0:T(8,128)(2,1)}) %reduce-scatter.22.cloned.1.call-update) | async-done | bytes 524304 | tf_op jit(solution)/shard_map/reduce_scatter | solution.py:455
  926.6 89.3 %reduce-scatter.18.cloned.1.call-done = bf16[64,3072]{1,0:T(8,128)(2,1)} async-done(((bf16[1024,3072]{1,0:T(8,128)(2,1)}), bf16[64,3072]{1,0:T(8,128)(2,1)}) %reduce-scatter.18.cloned.1.call-update) | async-done | bytes 393232 | tf_op jit(solution)/shard_map/reduce_scatter | solution.py:443
  1019.4 104.7 %reduce-scatter.26.cloned.1.call-done = bf16[256,1,1024]{0,2,1:T(8,128)(2,1)} async-done(((bf16[4096,1,1024]{0,2,1:T(8,128)(2,1)}), bf16[256,1,1024]{0,2,1:T(8,128)(2,1)}) %reduce-scatter.26.cloned.1.call-update) | async-done | bytes 524304 | tf_op jit(solution)/shard_map/reduce_scatter | solution.py:470
  1134.0 32.7 %all-reduce.5 = (bf16[1024]{0:T(1024)(128)(2,1)S(1)}, bf16[1024]{0:T(1024)(128)(2,1)S(1)}, bf16[1024]{0:T(1024)(128)(2,1)S(1)}, bf16[1024]{0:T(1024)(128)(2,1)S(1)}) all-reduce(bf16[1024]{0:T(1024)(128)(2,1)S(1)} %get-tuple-element.840, ...), channel_id=5, replica_groups=mesh['wide'=16,'narrow'=2] {'wide'}, use_global_device_ids=true, to_apply=%region_37.38.clone | all-reduce | flops 4096 | bytes 16384
  (311 shorter events, 213.2 us)
Async XLA Ops:
  7.2 131.1 %copy-start = (bf16[1024,1024]{1,0:T(8,128)(2,1)S(1)}, bf16[1024,1024]{1,0:T(8,128)(2,1)}, u32[]{:S(2)}) copy-start(bf16[1024,1024]{1,0:T(8,128)(2,1)} %param.39) | copy-start | bytes 6291460
  7.2 61.4 %all-gather.7.cloned.1.call-start = ((), (), s32[]{:S(2)}) async-start(), calls=%async_computation.19 | async-start | bytes 4456448 | tf_op jit(solution)/shard_map/all_gather | solution.py:118
  15.2 105.2 %all-gather.5.cloned.1.call-start = ((), (), s32[]{:S(2)}) async-start(), calls=%async_computation.18 | async-start | bytes 4456448 | tf_op jit(solution)/shard_map/all_gather | solution.py:117
  140.7 24.1 %all-to-all-start = ((bf16[2,1,80,1024]{3,2,1,0:T(8,128)(2,1)}), bf16[2,1,80,1024]{3,2,1,0:T(8,128)(2,1)}, u32[]{:S(2)}, u32[]{:S(2)}) async-start(bf16[2,1,80,1024]{3,2,1,0:T(8,128)(2,1)} %bitcast.56), calls=%async_computation | async-start | bytes 655360 | tf_op jit(solution)/shard_map/all_to_all | solution.py:201
  164.8 16.7 %all-to-all-start.2 = ((bf16[2,1,80,1024]{3,2,1,0:T(8,128)(2,1)}), bf16[2,1,80,1024]{3,2,1,0:T(8,128)(2,1)}, u32[]{:S(2)}, u32[]{:S(2)}) async-start(bf16[2,1,80,1024]{3,2,1,0:T(8,128)(2,1)} %bitcast.359), calls=%async_computation.2 | async-start | bytes 655360 | tf_op jit(solution)/shard_map/all_to_all | solution.py:237
  181.6 20.7 %all-to-all-start.1 = ((bf16[1,2,80,1024]{3,2,0,1:T(8,128)(2,1)}), bf16[1,2,80,1024]{3,2,0,1:T(8,128)(2,1)}, u32[]{:S(2)}, u32[]{:S(2)}) async-start(bf16[1,2,80,1024]{3,2,0,1:T(8,128)(2,1)} %fusion.89), calls=%async_computation.1 | async-start | bytes 655360 | tf_op jit(solution)/shard_map/all_to_all | solution.py:209
  202.3 10.8 all-to-all-start.3
  206.4 213.0 %reduce-scatter.28.cloned.1.call-start = ((), (), s32[]{:S(2)}) async-start(), calls=%async_computation.20 | async-start | bytes 8912896
  261.5 217.0 %reduce-scatter.30.cloned.1.call-start = ((), (), s32[]{:S(2)}) async-start(), calls=%async_computation.21 | async-start | bytes 278528
  263.5 273.3 %reduce-scatter.32.cloned.1.call-start = ((), (), s32[]{:S(2)}) async-start(), calls=%async_computation.22 | async-start | bytes 278528
  264.7 379.7 %reduce-scatter.34.cloned.1.call-start = ((), (), s32[]{:S(2)}) async-start(), calls=%async_computation.23 | async-start | bytes 8912896
  282.6 426.8 %reduce-scatter.20.cloned.1.call-start = ((), (), s32[]{:S(2)}) async-start(), calls=%async_computation.14 | async-start | bytes 2228224 | tf_op jit(solution)/shard_map/reduce_scatter | solution.py:446
  285.6 532.0 %reduce-scatter.24.cloned.1.call-start = ((), (), s32[]{:S(2)}) async-start(), calls=%async_computation.16 | async-start | bytes 8912896 | tf_op jit(solution)/shard_map/reduce_scatter | solution.py:458
  293.1 633.5 %reduce-scatter.22.cloned.1.call-start = ((), (), s32[]{:S(2)}) async-start(), calls=%async_computation.15 | async-start | bytes 8912896 | tf_op jit(solution)/shard_map/reduce_scatter | solution.py:455
  300.0 716.0 %reduce-scatter.18.cloned.1.call-start = ((), (), s32[]{:S(2)}) async-start(), calls=%async_computation.13 | async-start | bytes 6684672 | tf_op jit(solution)/shard_map/reduce_scatter | solution.py:443
  314.7 106.1 %copy-start.4 = (bf16[128,1,1024]{2,0,1:T(8,128)(2,1)S(1)}, bf16[128,1,1024]{2,0,1:T(8,128)(2,1)}, u32[]{:S(2)}) copy-start(bf16[128,1,1024]{2,0,1:T(8,128)(2,1)} %param.31) | copy-start | bytes 786436
  314.7 106.1 %copy-start.27 = (f32[1024]{0:T(1024)S(1)}, f32[1024]{0:T(1024)}, u32[]{:S(2)}) copy-start(f32[1024]{0:T(1024)} %param.36) | copy-start | bytes 12292
  314.7 106.1 %copy-start.28 = (f32[1024]{0:T(1024)S(1)}, f32[1024]{0:T(1024)}, u32[]{:S(2)}) copy-start(f32[1024]{0:T(1024)} %param.37) | copy-start | bytes 12292
  314.8 106.1 %copy-start.32 = (f32[128]{0:T(128)S(1)}, f32[128]{0:T(128)}, u32[]{:S(2)}) copy-start(f32[128]{0:T(128)} %copy-done.31) | copy-start | bytes 1540
  314.8 106.1 %copy-start.34 = (f32[128]{0:T(128)S(1)}, f32[128]{0:T(128)}, u32[]{:S(2)}) copy-start(f32[128]{0:T(128)} %copy-done.33) | copy-start | bytes 1540
  425.4 698.7 %reduce-scatter.26.cloned.1.call-start = ((), (), s32[]{:S(2)}) async-start(), calls=%async_computation.17 | async-start | bytes 8912896 | tf_op jit(solution)/shard_map/reduce_scatter | solution.py:470
  433.2 42.4 %copy-start.44 = (f32[2]{0:T(128)S(1)}, f32[2]{0:T(128)}, u32[]{:S(2)}) copy-start(f32[2]{0:T(128)} %param.35) | copy-start | bytes 28
  433.3 745.0 %all-reduce.10.cloned.1.call-start = ((), (), s32[]{:S(2)}) async-start(), calls=%async_computation.24 | async-start | bytes 3145728 | tf_op jit(solution)/shard_map/psum | solution.py:477
  1127.5 47.6 %copy-start.12 = (f32[128,1024]{1,0:T(8,128)S(1)}, f32[128,1024]{1,0:T(8,128)}, u32[]{:S(2)}) copy-start(f32[128,1024]{1,0:T(8,128)} %copy-done.11) | copy-start | bytes 1572868
  (45 other events, 195.1 us)
Sparse Core Ops, SparseCore 0:
  15.3 53.2 all-gather.6
  71.3 49.0 all-gather.4
  261.6 157.7 reduce-scatter.27
  423.4 55.0 reduce-scatter.29
  482.4 54.3 reduce-scatter.31
  540.7 103.6 reduce-scatter.33
  648.1 61.3 reduce-scatter.19
  714.0 103.5 reduce-scatter.23
  822.3 104.2 reduce-scatter.21
  930.9 84.9 reduce-scatter.17
  1020.0 104.0 reduce-scatter.25
  1126.4 51.8 all-reduce.9
where the time goes:
time: 1200 us; the launch traced here: 1190 us
  waiting for transfers between devices  825 us (69%)
  matrix products  116 us (10%)
  blocking collectives  101 us (8%)
  local copies, waits for them, and re-layouts  84 us (7%)
  other arithmetic  23.4 us (2%)
  starting transfers between devices  18 us (2%)
  between operations  15.9 us (1%)
    unnamed x16, waiting for transfers between devices  272 us
    reduce_scatter x1, waiting for transfers between devices, local(): lax.psum_scatter(dense_up_part.astype(jnp.bfloat16), 'wide', scatter_dime...  109 us
    reduce_scatter x1, waiting for transfers between devices, local(): lax.psum_scatter(dense_down_part.astype(jnp.bfloat16), 'wide', scatter_di...  108 us
    reduce_scatter x1, waiting for transfers between devices, local(): lax.psum_scatter(expert_down_part.astype(jnp.bfloat16), 'wide', scatter_d...  105 us
    reduce_scatter x1, waiting for transfers between devices, local(): lax.psum_scatter(project_in_part.astype(jnp.bfloat16), 'wide', scatter_di...  89.3 us
    reduce_scatter x1, waiting for transfers between devices, local(): lax.psum_scatter(project_out_part.astype(jnp.bfloat16), 'wide', scatter_d...  62.7 us
    unnamed x114, local copies, waits for them, and re-layouts  46.1 us
    all_gather x1, waiting for transfers between devices, local(): key_piece = lax.all_gather(key_rows, 'wide', axis=0, tiled=True)  45.6 us
  transfers between devices with their start and end apart: 16, of which 13 were waited for; matrix products, arithmetic and copies ran while one was open for 12% of the time, Pallas kernels for 0%

commit v1 on v0

v1 whole, which is shorter than its diff:
```python
import functools

import jax
import jax.numpy as jnp
from jax import lax
from jax.experimental import pallas as pl
from jax.experimental.pallas import tpu as pltpu
from jax.sharding import Mesh, PartitionSpec as P

HEADS = 16
HEAD_DIM = 64
WIDE = ("chip", "core")
ALL = ("chip", "core", "narrow")

score_scale = 0.125
norm_eps = 1e-05
momentum = 0.3
masked_score = -1e30
gelu_slope = 0.7978845608028654
gelu_cubic = 0.044715

f32 = jnp.float32
bf16 = jnp.bfloat16


def mm(left, right, dims=((1,), (0,))):
    return lax.dot_general(left, right, (dims, ((), ())), preferred_element_type=f32)


def norm_stats(rows):
    average = jnp.mean(rows, axis=-1, keepdims=True)
    centered = rows - average
    variance = jnp.mean(centered * centered, axis=-1, keepdims=True)
    rstd = lax.rsqrt(variance + norm_eps)
    return centered * rstd, rstd


def norm_back(grad, gain, normed, rstd):
    scaled = grad * gain
    mean_scaled = jnp.mean(scaled, axis=-1, keepdims=True)
    mean_product = jnp.mean(scaled * normed, axis=-1, keepdims=True)
    return rstd * (scaled - mean_scaled - normed * mean_product)


def gelu_pair(u):
    square = u * u
    t = jnp.tanh(gelu_slope * u * (1.0 + gelu_cubic * square))
    half = 0.5 * (1.0 + t)
    slope = half + 0.5 * u * (1.0 - t * t) * (gelu_slope * (1.0 + 3.0 * gelu_cubic * square))
    return u * half, slope


def three_parts(value):
    high = lax.reduce_precision(value, 8, 7)
    rest = value - high
    middle = lax.reduce_precision(rest, 8, 7)
    low = lax.reduce_precision(rest - middle, 8, 7)
    return high, middle, low


def span_columns(ref, first, block, per):
    return jnp.concatenate(
        [ref[block * per + t, first : first + HEAD_DIM, :] for t in range(per)], axis=1
    )


def rows_of(columns):
    return jnp.transpose(columns.astype(f32)).astype(bf16)


def iotas(span):
    shape = (span, span)
    return (
        lax.broadcasted_iota(jnp.int32, shape, 0),
        lax.broadcasted_iota(jnp.int32, shape, 1),
    )


def fold_rows(tile, op):
    return op(tile.reshape(tile.shape[0] // 8, 8, tile.shape[1]), axis=0)


def label_row(ref, block, per):
    return jnp.concatenate(
        [ref[block * per + t, 192:208, :].astype(f32)[0:1] for t in range(per)], axis=1
    )


def attend_kernel(span, per, qkv_ref, low_ref, wide_ref, lse_ref, key_s, label_s, score_s):
    blocks, _, rows = qkv_ref.shape
    count = blocks // per

    @pl.loop(0, blocks)
    def _(j):
        at = pl.ds(pl.multiple_of(j * rows, rows), rows)
        key_s[at, :] = rows_of(qkv_ref[j, 64:128, :])
        label_s[at, :] = jnp.transpose(qkv_ref[j, 192:208, :].astype(f32))

    row_at, column_at = iotas(span)

    @pl.loop(0, count)
    def _(i):
        query = (span_columns(qkv_ref, 0, i, per).astype(f32) * score_scale).astype(bf16)
        labels = label_row(qkv_ref, i, per)

        def score(j, peak):
            at = pl.ds(pl.multiple_of(j * span, span), span)
            s = mm(key_s[at, :], query)
            keep = (label_s[at, 0:1] == labels) & (j * span + row_at <= i * span + column_at)
            s = jnp.where(keep, s, masked_score)
            score_s[at, :] = s
            return jnp.maximum(peak, fold_rows(s, jnp.max))

        peak = lax.fori_loop(0, i + 1, score, jnp.full((8, span), masked_score, f32))
        peak = jnp.max(peak, axis=0, keepdims=True)

        def weigh(j, total):
            at = pl.ds(pl.multiple_of(j * span, span), span)
            e = jnp.exp(score_s[at, :] - peak)
            score_s[at, :] = e
            return total + fold_rows(e, jnp.sum)

        total = lax.fori_loop(0, i + 1, weigh, jnp.zeros((8, span), f32))
        total = jnp.sum(total, axis=0, keepdims=True)
        share = 1.0 / total

        def mix(j, out):
            at = pl.ds(pl.multiple_of(j * span, span), span)
            p = (score_s[at, :] * share).astype(bf16)
            return out + mm(span_columns(qkv_ref, 128, j, per), p)

        out = lax.fori_loop(0, i + 1, mix, jnp.zeros((HEAD_DIM, span), f32))
        for t in range(per):
            part = out[:, t * rows : (t + 1) * rows]
            wide_ref[i * per + t] = part
            low_ref[i * per + t] = part.astype(bf16)
        lse_ref[i] = peak + jnp.log(total)


def attend_back_kernel(
    span, per, qkv_ref, do_ref, wide_ref, lse_ref, out_ref, flat_ref,
    query_s, key_s, value_s, grad_s, label_s, delta_s, dq_s,
):
    blocks, _, rows = qkv_ref.shape
    count = blocks // per

    @pl.loop(0, blocks)
    def _(j):
        at = pl.ds(pl.multiple_of(j * rows, rows), rows)
        query_s[at, :] = rows_of(qkv_ref[j, 0:64, :])
        key_s[at, :] = rows_of(qkv_ref[j, 64:128, :])
        value_s[at, :] = rows_of(qkv_ref[j, 128:192, :])
        grad_s[at, :] = rows_of(do_ref[j])
        label_s[at, :] = jnp.transpose(qkv_ref[j, 192:208, :].astype(f32))
        delta_s[j] = jnp.sum(do_ref[j].astype(f32) * wide_ref[j], axis=0, keepdims=True)

    dq_s[...] = jnp.zeros_like(dq_s)
    row_at, column_at = iotas(span)

    @pl.loop(0, count)
    def _(j):
        at = pl.ds(pl.multiple_of(j * span, span), span)
        keys, values = key_s[at, :], value_s[at, :]
        key_columns = span_columns(qkv_ref, 64, j, per)
        key_labels = label_s[at, 0:1]

        def step(i, carry):
            dk, dv = carry
            to = pl.ds(pl.multiple_of(i * span, span), span)
            query = (span_columns(qkv_ref, 0, i, per).astype(f32) * score_scale).astype(bf16)
            grad = jnp.concatenate([do_ref[i * per + t] for t in range(per)], axis=1)
            delta = jnp.concatenate([delta_s[i * per + t] for t in range(per)], axis=1)
            labels = label_row(qkv_ref, i, per)
            s = mm(keys, query)
            keep = (key_labels == labels) & (j * span + row_at <= i * span + column_at)
            p = jnp.where(keep, jnp.exp(s - lse_ref[i]), 0.0)
            dp = mm(values, grad)
            ds = (p * (dp - delta)).astype(bf16)
            dq_s[i] = dq_s[i] + mm(key_columns, ds)
            dk = dk + mm(ds, query_s[to, :])
            dv = dv + mm(p.astype(bf16), grad_s[to, :])
            return dk, dv

        zero = jnp.zeros((span, HEAD_DIM), f32)
        dk, dv = lax.fori_loop(j, count, step, (zero, zero))
        dk = jnp.transpose(dk * score_scale).astype(bf16)
        dv = jnp.transpose(dv).astype(bf16)
        flat_ref[64:128, at] = dk
        flat_ref[128:192, at] = dv
        for t in range(per):
            part = slice(t * rows, (t + 1) * rows)
            out_ref[j * per + t, 64:128, :] = dk[:, part]
            out_ref[j * per + t, 128:192, :] = dv[:, part]

    @pl.loop(0, count)
    def _(i):
        at = pl.ds(pl.multiple_of(i * span, span), span)
        dq = (dq_s[i] * score_scale).astype(bf16)
        flat_ref[0:64, at] = dq
        for t in range(per):
            out_ref[i * per + t, 0:64, :] = dq[:, t * rows : (t + 1) * rows]


def attend(qkv):
    blocks, _, rows = qkv.shape
    per = max(1, 256 // rows)
    span, length = per * rows, blocks * rows
    return pl.pallas_call(
        functools.partial(attend_kernel, span, per),
        out_shape=(
            jax.ShapeDtypeStruct((blocks, HEAD_DIM, rows), bf16),
            jax.ShapeDtypeStruct((blocks, HEAD_DIM, rows), f32),
            jax.ShapeDtypeStruct((length // span, 1, span), f32),
        ),
        scratch_shapes=[
            pltpu.VMEM((length, HEAD_DIM), bf16),
            pltpu.VMEM((length, 16), f32),
            pltpu.VMEM((length, span), f32),
        ],
        compiler_params=pltpu.CompilerParams(vmem_limit_bytes=24 * 2**20),
        cost_estimate=pl.CostEstimate(
            flops=length * length * HEAD_DIM * 2,
            bytes_accessed=length * 1024,
            transcendentals=length * length // 2,
        ),
        name="attend",
    )(qkv)


def attend_back(qkv, grad, wide, lse):
    blocks, _, rows = qkv.shape
    per = max(1, 256 // rows)
    span, length = per * rows, blocks * rows
    return pl.pallas_call(
        functools.partial(attend_back_kernel, span, per),
        out_shape=(
            jax.ShapeDtypeStruct((blocks, 3 * HEAD_DIM, rows), bf16),
            jax.ShapeDtypeStruct((3 * HEAD_DIM, length), bf16),
        ),
        scratch_shapes=[
            pltpu.VMEM((length, HEAD_DIM), bf16),
            pltpu.VMEM((length, HEAD_DIM), bf16),
            pltpu.VMEM((length, HEAD_DIM), bf16),
            pltpu.VMEM((length, HEAD_DIM), bf16),
            pltpu.VMEM((length, 16), f32),
            pltpu.VMEM((blocks, 1, rows), f32),
            pltpu.VMEM((length // span, HEAD_DIM, span), f32),
        ],
        compiler_params=pltpu.CompilerParams(vmem_limit_bytes=32 * 2**20),
        cost_estimate=pl.CostEstimate(
            flops=length * length * HEAD_DIM * 5,
            bytes_accessed=length * 2048,
            transcendentals=length * length // 2,
        ),
        name="attend_back",
    )(qkv, grad, wide, lse)


def feed_kernel(rows_ref, grad_ref, up_ref, down_ref, out_ref, back_ref):
    step = pl.program_id(0)
    up, down = up_ref[...], down_ref[...]
    act, slope = gelu_pair(mm(rows_ref[...], up))
    out = mm(act.astype(bf16), down)
    inner = (mm(grad_ref[...], down, ((1,), (1,))) * slope).astype(bf16)
    back = mm(inner, up, ((1,), (1,)))

    @pl.when(step == 0)
    def _():
        out_ref[...] = out
        back_ref[...] = back

    @pl.when(step > 0)
    def _():
        out_ref[...] += out
        back_ref[...] += back


def feed(rows, grad, up, down):
    count, width = rows.shape
    hidden = up.shape[1]
    chunk = min(hidden, 512)
    whole = pl.BlockSpec((count, width), lambda c: (0, 0))
    return pl.pallas_call(
        feed_kernel,
        grid=(hidden // chunk,),
        in_specs=[
            whole,
            whole,
            pl.BlockSpec((width, chunk), lambda c: (0, c)),
            pl.BlockSpec((chunk, width), lambda c: (c, 0)),
        ],
        out_specs=[whole, whole],
        out_shape=[jax.ShapeDtypeStruct((count, width), f32)] * 2,
        compiler_params=pltpu.CompilerParams(vmem_limit_bytes=24 * 2**20),
        cost_estimate=pl.CostEstimate(
            flops=8 * count * width * hidden,
            bytes_accessed=4 * width * hidden,
            transcendentals=count * hidden,
        ),
        name="feed",
    )(rows, grad, up, down)


def slice_kernel(
    steps, expert_units, mine_ref, rows_ref, grad_ref, up_ref, down_ref, up_out, down_out, up_acc, down_acc
):
    step = pl.program_id(0)
    count = grad_ref.shape[1]

    @pl.when(step == 0)
    def _():
        up_acc[...] = jnp.zeros_like(up_acc)
        down_acc[...] = jnp.zeros_like(down_acc)

    rows, dense_grad, expert_grad = [], [], []
    for t in range(rows_ref.shape[0]):
        scalars = jnp.transpose(rows_ref[t, count : count + 8, 0:count].astype(f32))
        mixing = scalars[:, 0:1] + scalars[:, 1:2] + scalars[:, 2:3]
        gate = scalars[:, 3:4] + scalars[:, 4:5] + scalars[:, 5:6]
        mine = scalars[:, 6:7] == mine_ref[0].astype(f32)
        grad = grad_ref[t].astype(f32)
        rows.append(rows_ref[t, 0:count, :])
        dense_grad.append((mixing * grad).astype(bf16))
        expert_grad.append((jnp.where(mine, gate, 0.0) * grad).astype(bf16))
    rows = jnp.concatenate(rows, axis=0)
    dense_grad = jnp.concatenate(dense_grad, axis=0)
    expert_grad = jnp.concatenate(expert_grad, axis=0)
    act, slope = gelu_pair(mm(rows, up_ref[...]))
    act = act.astype(bf16)
    inner = jnp.concatenate(
        [mm(expert_grad, down_ref[:, :expert_units]), mm(dense_grad, down_ref[:, expert_units:])],
        axis=1,
    )
    inner = (inner * slope).astype(bf16)
    first = ((0,), (0,))
    up_acc[...] += mm(inner, rows, first)
    down_acc[:expert_units, :] += mm(act[:, :expert_units], expert_grad, first)
    down_acc[expert_units:, :] += mm(act[:, expert_units:], dense_grad, first)

    @pl.when(step == steps - 1)
    def _():
        up_out[...] = jnp.transpose(up_acc[...]).astype(bf16)
        down_out[...] = down_acc[...]


def slice_grads(mine, rows, grad, up, down, expert_units):
    devices, padded, width = rows.shape
    count = grad.shape[1]
    units = up.shape[1]
    per = 2
    steps = devices // per
    fixed = pl.BlockSpec((width, units), lambda c, m: (0, 0))
    return pl.pallas_call(
        functools.partial(slice_kernel, steps, expert_units),
        grid_spec=pltpu.PrefetchScalarGridSpec(
            num_scalar_prefetch=1,
            grid=(steps,),
            in_specs=[
                pl.BlockSpec((per, padded, width), lambda c, m: (c, 0, 0)),
                pl.BlockSpec((per, count, width), lambda c, m: (c, 0, 0)),
                fixed,
                fixed,
            ],
            out_specs=[
                pl.BlockSpec((width, units), lambda c, m: (0, 0)),
                pl.BlockSpec((units, width), lambda c, m: (0, 0)),
            ],
            scratch_shapes=[pltpu.VMEM((units, width), f32), pltpu.VMEM((units, width), f32)],
        ),
        out_shape=[
            jax.ShapeDtypeStruct((width, units), bf16),
            jax.ShapeDtypeStruct((units, width), f32),
        ],
        compiler_params=pltpu.CompilerParams(vmem_limit_bytes=32 * 2**20),
        cost_estimate=pl.CostEstimate(
            flops=8 * devices * count * width * units,
            bytes_accessed=4 * devices * count * width,
            transcendentals=devices * count * units,
        ),
        name="slice_grads",
    )(mine, rows, grad, up, down)


def gather(value):
    return lax.all_gather(value, WIDE, axis=0, tiled=True)


def exchange(columns):
    wide = lax.axis_size("chip") * lax.axis_size("core")
    blocks = columns.astype(bf16).reshape(wide, columns.shape[0] // wide, columns.shape[1])
    got = lax.all_to_all(blocks, WIDE, 0, 0, tiled=True)
    return got.transpose(1, 0, 2).reshape(blocks.shape[1], wide * blocks.shape[2])


def plain_slice(rows, grad, up, down):
    act, slope = gelu_pair(mm(rows, up))
    inner = (mm(grad, down, ((1,), (1,))) * slope).astype(bf16)
    return mm(rows, inner, ((0,), (0,))), mm(act.astype(bf16), grad, ((0,), (0,)))


def other_narrow(value):
    size = lax.axis_size("narrow")
    if size != 2:
        return lax.all_gather(value, "narrow", axis=0, tiled=False)
    swapped = lax.ppermute(value, "narrow", [(0, 1), (1, 0)])
    first = lax.axis_index("narrow") == 0
    return jnp.stack([jnp.where(first, value, swapped), jnp.where(first, swapped, value)])


def local(
    tokens, document, routing, capacity, load_before, first_gain, first_shift, project_in,
    project_out, second_gain, second_shift, dense_up, dense_down, router, mixer, mixer_bias,
    expert_up, expert_down, cotangent,
):
    rows, seq_count, width = tokens.shape
    assert seq_count == 1 and width == HEADS * HEAD_DIM
    wide, narrow = lax.axis_size("chip") * lax.axis_size("core"), lax.axis_size("narrow")
    devices = wide * narrow
    experts = capacity.shape[0]
    hidden_units = dense_up.shape[1]
    assert experts == narrow and wide % HEADS == 0
    copies = wide // HEADS
    my_wide = lax.axis_index("chip") * lax.axis_size("core") + lax.axis_index("core")
    my_narrow = lax.axis_index("narrow")

    inputs = tokens.reshape(rows, width).astype(f32)
    grad_low = cotangent.reshape(rows, width)
    grad_out = grad_low.astype(f32)
    gather_all = devices * rows * width <= 2**23
    if gather_all:
        grad_all = lax.all_gather(grad_low, ALL, axis=0, tiled=False)

    normed_one, rstd_one = norm_stats(inputs)
    a = (normed_one * first_gain + first_shift).astype(bf16)
    projected = mm(a, project_in).astype(bf16)
    a_all = lax.all_gather(a, WIDE, axis=0, tiled=True)
    by_head = projected.reshape(rows, 3, HEADS, HEAD_DIM).transpose(2, 1, 3, 0)
    by_head = by_head.reshape(HEADS, 3 * HEAD_DIM, rows)
    labels = jnp.broadcast_to(document.reshape(1, 1, rows).astype(bf16), (HEADS, 16, rows))
    payload = jnp.concatenate([by_head, labels], axis=1)
    payload = jnp.repeat(payload, copies, axis=0)
    qkv = lax.all_to_all(payload, WIDE, 0, 0, tiled=True)
    head_low, head_wide, lse = attend(qkv)
    attended = lax.all_to_all(head_low, WIDE, 0, 0, tiled=True)[::copies].reshape(width, rows)

    hidden = inputs + mm(attended, project_out, ((0,), (0,)))
    normed_two, rstd_two = norm_stats(hidden)
    b = (normed_two * second_gain + second_shift).astype(bf16)

    def scores_of(values):
        gates = jax.nn.softmax(mm(values, router), axis=-1)
        mixing = jax.nn.softmax(mm(values, mixer) + mixer_bias, axis=-1)
        return gates, mixing

    gates, mixing = scores_of(b)
    chosen = routing.reshape(rows)
    onehot = (chosen[:, None] == jnp.arange(experts, dtype=jnp.int32)[None, :]).astype(jnp.int32)
    chosen_gate = jnp.sum(gates * onehot, axis=-1, keepdims=True)
    earlier = jnp.cumsum(onehot, axis=0) - onehot
    slot_rank = jnp.sum(earlier * onehot, axis=-1)
    kept = slot_rank < jnp.sum(capacity[None, :] * onehot, axis=-1)
    counts = jnp.sum(onehot * kept[:, None].astype(jnp.int32), axis=0)
    slots = rows * 5 // (4 * experts)
    slot_index = chosen * slots + slot_rank
    dispatch = (
        (slot_index[None, :] == jnp.arange(experts * slots, dtype=jnp.int32)[:, None])
        & kept[None, :]
    ).astype(bf16)

    def send_slots(values):
        filled = mm(dispatch, values).astype(bf16).reshape(experts, slots, width)
        return lax.all_to_all(filled, "narrow", 0, 0, tiled=True).reshape(narrow * slots, width)

    slot_grad = send_slots(grad_low)
    slot_rows = send_slots(b)

    own = width // wide
    code = jnp.where(kept, chosen, experts).astype(f32)
    scalars = jnp.stack(
        [*three_parts(mixing[:, 0]), *three_parts(mixing[:, 1] * chosen_gate[:, 0]), code, code]
    )
    scalars = jnp.pad(scalars.astype(bf16), ((0, 0), (0, width - rows)))
    if gather_all:
        rows_all = lax.all_gather(jnp.concatenate([b, scalars]), ALL, axis=0, tiled=False)

    dense_grad = (mixing[:, :1] * grad_out).astype(bf16)
    dense_res, dense_back = feed(b, dense_grad, dense_up, dense_down)

    my_up = expert_up.reshape(width, hidden_units)
    my_down = expert_down.reshape(hidden_units, width)
    slot_gates, slot_mixing = scores_of(slot_rows)
    slot_gate = lax.dynamic_index_in_dim(slot_gates, my_narrow, axis=1)
    slot_back = (slot_gate * (slot_mixing[:, 1:] * slot_grad.astype(f32))).astype(bf16)
    slot_out, slot_rows_grad = feed(slot_rows, slot_back, my_up, my_down)
    results = jnp.concatenate(
        [
            slot_out.astype(bf16).reshape(narrow, slots, width),
            slot_rows_grad.astype(bf16).reshape(narrow, slots, width),
        ],
        axis=1,
    )
    returned = lax.all_to_all(results, "narrow", 0, 0, tiled=True)

    def from_slots(values):
        return mm(dispatch, values.reshape(experts * slots, width), ((0,), (0,)))

    expert_raw = from_slots(returned[:, :slots])
    expert_back = from_slots(returned[:, slots:])
    expert_res = chosen_gate * expert_raw
    output = hidden + mixing[:, :1] * dense_res + mixing[:, 1:] * expert_res
    result = output.astype(bf16).reshape(rows, 1, width)

    grad_gate = jnp.sum(mixing[:, 1:] * grad_out * expert_raw, axis=-1, keepdims=True)
    grad_mixing = jnp.concatenate(
        [
            jnp.sum(grad_out * dense_res, axis=-1, keepdims=True),
            jnp.sum(grad_out * expert_res, axis=-1, keepdims=True),
        ],
        axis=-1,
    )
    grad_mix_logits = mixing * (grad_mixing - jnp.sum(mixing * grad_mixing, axis=-1, keepdims=True))
    grad_router_logits = gates * (onehot.astype(f32) - chosen_gate) * grad_gate
    grad_b = dense_back + expert_back
    for e in range(experts):
        grad_b = grad_b + grad_router_logits[:, e : e + 1] * router[:, e].astype(f32)[None, :]
    for e in range(2):
        grad_b = grad_b + grad_mix_logits[:, e : e + 1] * mixer[:, e].astype(f32)[None, :]
    logit_grads = jnp.concatenate([grad_router_logits, grad_mix_logits], axis=1)
    small_part = jnp.einsum(
        "nd,ne->de", b.astype(f32), logit_grads, precision=lax.Precision.HIGHEST
    )
    second_gain_part = jnp.sum(grad_b * normed_two, axis=0)
    second_shift_part = jnp.sum(grad_b, axis=0)
    grad_hidden = grad_out + norm_back(grad_b, second_gain, normed_two, rstd_two)
    grad_attn = grad_hidden.astype(bf16)

    grad_heads = mm(project_out, grad_attn, ((1,), (1,))).astype(bf16)
    grad_heads = grad_heads.reshape(HEADS, HEAD_DIM, rows)
    grad_heads = jnp.repeat(grad_heads, copies, axis=0)
    head_grad = lax.all_to_all(grad_heads, WIDE, 0, 0, tiled=True)
    grad_blocks, grad_flat = attend_back(qkv, head_grad, head_wide, lse)
    sent_back = lax.all_to_all(grad_blocks, WIDE, 0, 0, tiled=True)[::copies]
    grad_qkv = sent_back.reshape(HEADS, 3, HEAD_DIM, rows).transpose(1, 0, 2, 3)
    grad_qkv = grad_qkv.reshape(3 * width, rows)
    grad_a = mm(grad_qkv, project_in, ((0,), (1,)))
    first_gain_part = jnp.sum(grad_a * normed_one, axis=0)
    first_shift_part = jnp.sum(grad_a, axis=0)
    input_grad = grad_hidden + norm_back(grad_a, first_gain, normed_one, rstd_one)
    input_grad = input_grad.astype(bf16).reshape(rows, 1, width)

    chips, cores = lax.axis_size("chip"), lax.axis_size("core")
    assert cores == 2
    core = lax.axis_index("core")
    out_part = mm(attended, grad_attn).reshape(chips, cores, own, width)
    swap = [(0, 1), (1, 0)]
    mine = lax.dynamic_index_in_dim(out_part, core, axis=1, keepdims=False)
    theirs = lax.dynamic_index_in_dim(out_part, 1 - core, axis=1, keepdims=False)
    out_pair = mine + lax.ppermute(theirs.astype(bf16), "core", swap).astype(f32)
    out_blocks = lax.all_to_all(out_pair.astype(bf16), "chip", 0, 0, tiled=True)
    out_sum = jnp.sum(out_blocks.astype(f32), axis=0)
    project_out_grad = jnp.sum(other_narrow(out_sum.astype(bf16)).astype(f32), axis=0)

    expert_units, dense_units = hidden_units // wide, hidden_units // devices
    up_slice = lax.dynamic_slice_in_dim(my_up, my_wide * expert_units, expert_units, axis=1)
    down_slice = lax.dynamic_slice_in_dim(my_down, my_wide * expert_units, expert_units, axis=0)
    if gather_all:
        lanes = -(-dense_units // 128) * 128
        dense_first = my_wide * expert_units + my_narrow * dense_units
        dense_up_slice = lax.dynamic_slice_in_dim(dense_up, dense_first, dense_units, axis=1)
        dense_down_slice = lax.dynamic_slice_in_dim(dense_down, dense_first, dense_units, axis=0)
        fill = ((0, 0), (0, lanes - dense_units))
        ups = jnp.concatenate([up_slice, jnp.pad(dense_up_slice, fill)], axis=1)
        downs = jnp.concatenate([down_slice.T, jnp.pad(dense_down_slice.T, fill)], axis=1)
        ups_part, downs_part = slice_grads(
            my_narrow.astype(jnp.int32).reshape(1), rows_all, grad_all, ups, downs, expert_units
        )
        expert_down_grad = downs_part[:expert_units].reshape(expert_units, 1, width)
        dense_down_part = downs_part[expert_units : expert_units + dense_units].astype(bf16)
        dense_down_grad = other_narrow(dense_down_part).astype(f32)
        dense_down_grad = dense_down_grad.reshape(narrow * dense_units, width)
        ups_blocks = ups_part[:, : expert_units + dense_units].reshape(wide, own, -1)
        ups_got = lax.all_to_all(ups_blocks, WIDE, 0, 0, tiled=True)
        expert_up_grad = ups_got[:, :, :expert_units].transpose(1, 0, 2).astype(f32)
        expert_up_grad = expert_up_grad.reshape(own, 1, hidden_units)
        dense_got = other_narrow(ups_got[:, :, expert_units:])
        dense_up_grad = dense_got.transpose(2, 1, 0, 3).reshape(own, hidden_units).astype(f32)
    else:
        dense_up_slice = lax.dynamic_slice_in_dim(
            dense_up, my_wide * expert_units, expert_units, axis=1
        )
        dense_down_slice = lax.dynamic_slice_in_dim(
            dense_down, my_wide * expert_units, expert_units, axis=0
        )
        dense_up_part, dense_down_part = plain_slice(
            gather(b), gather(dense_grad), dense_up_slice, dense_down_slice
        )
        dense_down_grad = lax.psum(dense_down_part.astype(bf16), "narrow").astype(f32)
        dense_up_grad = lax.psum(exchange(dense_up_part), "narrow").astype(f32)
        expert_up_part, expert_down_grad = plain_slice(
            gather(slot_rows), gather(slot_back), up_slice, down_slice
        )
        expert_down_grad = expert_down_grad.reshape(expert_units, 1, width)
        expert_up_grad = exchange(expert_up_part).astype(f32).reshape(own, 1, hidden_units)

    in_part = mm(grad_flat, a_all).astype(bf16)
    half = 3 * HEAD_DIM // 2
    in_blocks = in_part.reshape(2, half, wide, own).transpose(2, 1, 0, 3)
    in_blocks = in_blocks.reshape(wide, half * 2 * own // 128, 128)
    bias_parts = jnp.stack(three_parts(jnp.sum(grad_mix_logits, axis=0))).reshape(1, 6)
    vectors = jnp.stack([first_gain_part, first_shift_part, second_gain_part, second_shift_part])
    vectors = vectors.reshape(4, wide, own).transpose(1, 0, 2).reshape(wide, 4 * own)
    small = small_part.reshape(wide, own * (experts + 2))
    flat = jnp.concatenate([vectors, small, jnp.broadcast_to(bias_parts, (wide, 6))], axis=1)
    short = -(-flat.shape[1] // 2048) * 2048
    flat = jnp.pad(flat, ((0, 0), (0, short - flat.shape[1]))).astype(bf16)
    both = jnp.concatenate([in_blocks, flat.reshape(wide, short // 128, 128)], axis=1)
    both = jnp.broadcast_to(both[:, None], (wide, narrow) + both.shape[1:])
    both = both.reshape((devices,) + both.shape[2:])
    got = lax.all_to_all(both, ALL, 0, 0, tiled=True)
    got = got.reshape((wide, narrow) + got.shape[1:])
    in_rows = in_blocks.shape[1]
    in_sum = jnp.sum(got[::copies, :, :in_rows].astype(f32), axis=1)
    in_sum = in_sum.reshape(HEADS, half, 2, own).transpose(0, 2, 1, 3)
    in_sum = in_sum.reshape(HEADS, 3, HEAD_DIM, own).transpose(3, 1, 0, 2)
    project_in_grad = in_sum.reshape(own, 3 * width)
    sums = jnp.sum(got[:, :, in_rows:].astype(f32), axis=(0, 1)).reshape(short)
    vector_sums = sums[: 4 * own].reshape(4, own)
    small_sum = sums[4 * own : own * (6 + experts)].reshape(own, experts + 2)
    bias_at = own * (6 + experts)
    mixer_bias_grad = jnp.sum(sums[bias_at : bias_at + 6].reshape(3, 2), axis=0)

    if gather_all:
        codes = rows_all[:, rows + 6, :rows].astype(f32).reshape(devices * rows, 1)
        count_sum = jnp.sum((codes == jnp.arange(experts, dtype=f32)[None, :]).astype(f32), axis=0)
    else:
        count_sum = lax.psum(counts.astype(f32), ALL)
    load_after = momentum * load_before + (1.0 - momentum) * (
        count_sum * experts / (devices * rows)
    )
    return (
        result,
        input_grad,
        vector_sums[0],
        vector_sums[1],
        project_in_grad,
        project_out_grad,
        vector_sums[2],
        vector_sums[3],
        dense_up_grad,
        dense_down_grad,
        small_sum[:, :experts],
        small_sum[:, experts:],
        mixer_bias_grad,
        expert_up_grad,
        expert_down_grad,
        load_after,
    )


def solution(mesh):
    wide, narrow = mesh.devices.shape
    fine = Mesh(mesh.devices.reshape(wide // 2, 2, narrow), ALL)
    by_token = P(WIDE, "narrow", None)
    by_expert = P(None, "narrow", None)
    return jax.shard_map(
        local,
        mesh=fine,
        in_specs=(
            by_token, P(WIDE, "narrow"), by_token, P(), P(), P(), P(), P(), P(), P(), P(), P(),
            P(), P(), P(), P(), by_expert, by_expert, by_token,
        ),
        out_specs=(
            by_token, by_token, P(WIDE), P(WIDE), P(WIDE, None), P(WIDE, None), P(WIDE), P(WIDE),
            P(WIDE, None), P(WIDE, None), P(WIDE, None), P(WIDE, None), P(), by_token, by_token,
            P(),
        ),
        check_vma=False,
    )
```

time: 1200 us -> 396 us (0.33)
  waiting for transfers between devices: 825 us -> 101 us
  matrix products: 116 us -> 22.1 us
  Pallas kernels: 0 us -> 85.6 us
  blocking collectives: 101 us -> 34.4 us
  starting transfers between devices: 18 us -> 53.8 us
  local copies, waits for them, and re-layouts: 84 us -> 60.4 us
    reduce_scatter x5 -> x0, waiting for transfers between devices: 474 us -> none  [the longest x1 109 us: local(): lax.psum_scatter(dense_up_part.astype(jnp.bfloat16), 'wide', scatter_dime...]
    unnamed x16 -> x3, waiting for transfers between devices: 272 us -> 0.73 us
    dot_general x35 -> x15, matrix products: 116 us -> 22.1 us  [the longest x14 21.9 us: mm(): lax.dot_general(left, right, (dims, ((), ())), preferred_element_type=f32)]
    pallas_call x0 -> x5, Pallas kernels: none -> 85.6 us  [the longest x2 25.5 us: feed(): pl.pallas_call(feed_kernel, grid=(hidden // chunk,), in_specs=[whole, who...]
    all_to_all x4 -> x9, waiting for transfers between devices: 4.23 us -> 85.5 us  [the longest x1 21.7 us: local(): sent_back = lax.all_to_all(grad_blocks, WIDE, 0, 0, tiled=True)[::copies]]
    all_gather x2 -> x3, waiting for transfers between devices: 73.9 us -> 0.02 us  [the longest x1 0.02 us: local(): a_all = lax.all_gather(a, WIDE, axis=0, tiled=True)]
    psum x2 -> x0, blocking collectives: 45.4 us -> none  [the longest x1 40.4 us: local(): lax.psum((counts.astype(jnp.float32), mixer_bias_part), ('wide', 'narrow'))]
    all_to_all x0 -> x1, blocking collectives: none -> 34.4 us  [local(): qkv = lax.all_to_all(payload, WIDE, 0, 0, tiled=True)]
  transfers between devices with their start and end apart: 16 -> 16, of which waited for: 13 -> 12; matrix products, arithmetic and copies ran while one was open for 12% -> 18% of each run, Pallas kernels for 0% -> 16%
where the time goes in v1:
time: 396 us; the launch traced here: 394 us
  waiting for transfers between devices  101 us (26%)
  Pallas kernels  85.6 us (22%)
  local copies, waits for them, and re-layouts  60.4 us (15%)
  starting transfers between devices  53.8 us (14%)
  blocking collectives  34.4 us (9%)
  other arithmetic  22.3 us (6%)
  matrix products  22.1 us (6%)
  between operations  14.7 us (4%)
    all_to_all x1, blocking collectives, local(): qkv = lax.all_to_all(payload, WIDE, 0, 0, tiled=True)  34.4 us
    unnamed x88, local copies, waits for them, and re-layouts  31.6 us
    pallas_call x2, Pallas kernels, feed(): pl.pallas_call(feed_kernel, grid=(hidden // chunk,), in_specs=[whole, who...  25.5 us
    pallas_call x1, Pallas kernels, slice_grads(): pl.pallas_call(functools.partial(slice_kernel, steps, expert_units), grid...  24.2 us
    dot_general x14, matrix products, mm(): lax.dot_general(left, right, (dims, ((), ())), preferred_element_type=f32)  21.9 us
    all_to_all x1, waiting for transfers between devices, local(): sent_back = lax.all_to_all(grad_blocks, WIDE, 0, 0, tiled=True)[::copies]  21.7 us
    pallas_call x1, Pallas kernels, attend_back(): pl.pallas_call(functools.partial(attend_back_kernel, span, per), out_shap...  19.6 us
    pallas_call x1, Pallas kernels, attend(): pl.pallas_call(functools.partial(attend_kernel, span, per), out_shape=(ja...  16.4 us
  transfers between devices with their start and end apart: 16, of which 12 were waited for; matrix products, arithmetic and copies ran while one was open for 18% of the time, Pallas kernels for 16%

profile of v1, /device:TPU:0, one launch (start us, length us, event | category | flops | bytes accessed | tf_op | source)
XLA Modules:
  0.0 394.1 jit_solution(17969798851881072850)
XLA Ops:
  12.3 3.9 convolution_convert_fusion
  18.7 34.4 %all_to_all.50.qkv_ref = bf16[16,208,128]{2,1,0:T(8,128)(2,1)S(1)} all-to-all(bf16[16,208,128]{2,1,0:T(8,128)(2,1)S(1)} %pad_maximum_fusion), channel_id=1, replica_groups=mesh['chip'=8,'core'=2,'narrow'=2] {'chip','core'}, dimensions={0} | all-to-all | bytes 1703936 | tf_op jit(solution)/shard_map/all_to_all | solution.py:442
  53.1 16.4 %attend.1 = (bf16[16,64,128]{2,1,0:T(8,128)(2,1)}, f32[16,64,128]{2,1,0:T(8,128)S(1)}, f32[8,1,256]{2,1,0:T(1,128)S(1)}) custom-call(bf16[16,208,128]{2,1,0:T(8,128)(2,1)S(1)} %all_to_all.50.qkv_ref), custom_call_target="tpu_custom_call" | custom-call | flops 536870912 | bytes 2097152 | tf_op jit(solution)/shard_map/attend/pallas_call | solution.py:208
  71.1 10.1 %all-to-all-start.1 = ((bf16[16,64,128]{2,1,0:T(8,128)(2,1)}), bf16[16,64,128]{2,1,0:T(8,128)(2,1)S(1)}, u32[]{:S(2)}, u32[]{:S(2)}) async-start(bf16[16,64,128]{2,1,0:T(8,128)(2,1)} %get-tuple-element.27), calls=%async_computation.1 | async-start | bytes 524288 | tf_op jit(solution)/shard_map/all_to_all | solution.py:444
  81.8 11.7 %all-to-all-done.1 = bf16[16,64,128]{2,1,0:T(8,128)(2,1)S(1)} async-done(((bf16[16,64,128]{2,1,0:T(8,128)(2,1)}), bf16[16,64,128]{2,1,0:T(8,128)(2,1)S(1)}, u32[]{:S(2)}, u32[]{:S(2)}) %all-to-all-start.1) | async-done | bytes 262176 | tf_op jit(solution)/shard_map/all_to_all | solution.py:444
  101.9 7.0 %all-to-all-done.2 = bf16[2,80,1024]{2,1,0:T(8,128)(2,1)S(1)} async-done(((bf16[2,80,1024]{2,1,0:T(8,128)(2,1)}), bf16[2,80,1024]{2,1,0:T(8,128)(2,1)S(1)}, u32[]{:S(2)}, u32[]{:S(2)}) %all-to-all-start.2) | async-done | bytes 327712 | tf_op jit(solution)/shard_map/all_to_all | solution.py:472
  112.9 5.0 %all-to-all-done.3 = bf16[2,80,1024]{2,1,0:T(8,128)(2,1)S(1)} async-done(((bf16[2,80,1024]{2,1,0:T(8,128)(2,1)}), bf16[2,80,1024]{2,1,0:T(8,128)(2,1)S(1)}, u32[]{:S(2)}, u32[]{:S(2)}) %all-to-all-start.3) | async-done | bytes 327712 | tf_op jit(solution)/shard_map/all_to_all | solution.py:472
  124.9 13.2 %feed.3 = (f32[160,1024]{1,0:T(8,128)S(1)}, f32[160,1024]{1,0:T(8,128)S(1)}) custom-call(bf16[160,1024]{1,0:T(8,128)(2,1)S(1)} %bitcast.237, bf16[160,1024]{1,0:T(8,128)(2,1)S(1)} %fusion.9.grad_ref, bf16[1024,4096]{1,0:T(8,128)(2,1)S(1)} %bitcast.239, bf16[4096,1024]{1,0:T(8,128)(2,1)S(1)} %bitcast.238), custom_call_target="tpu_custom_call" | custom-call | flops 5368709120 | bytes 16777216 | tf_op jit(solution)/shard_map/feed/pallas_call | solution.py:283
  139.1 4.3 %all-to-all-start.4 = ((bf16[2,160,1024]{2,1,0:T(8,128)(2,1)}), bf16[2,160,1024]{2,1,0:T(8,128)(2,1)}, u32[]{:S(2)}, u32[]{:S(2)}) async-start(bf16[2,160,1024]{2,1,0:T(8,128)(2,1)} %pad_maximum_fusion.3), calls=%async_computation.4 | async-start | bytes 1310720 | tf_op jit(solution)/shard_map/all_to_all | solution.py:502
  150.4 12.3 %feed.2 = (f32[128,1024]{1,0:T(8,128)S(1)}, f32[128,1024]{1,0:T(8,128)S(1)}) custom-call(bf16[128,1024]{1,0:T(8,128)(2,1)S(1)} %add_convert_fusion.1.rows_ref, bf16[128,1024]{1,0:T(8,128)(2,1)S(1)} %fusion.26.grad_ref, bf16[1024,4096]{1,0:T(8,128)(2,1)S(1)} %copy-done.3, bf16[4096,1024]{1,0:T(8,128)(2,1)S(1)} %copy-done.2), custom_call_target="tpu_custom_call" | custom-call | flops 4294967296 | bytes 16777216 | tf_op jit(solution)/shard_map/feed/pallas_call | solution.py:283
  171.2 4.5 %all-to-all-start.5 = ((bf16[16,64,128]{2,1,0:T(8,128)(2,1)}), bf16[16,64,128]{2,1,0:T(8,128)(2,1)S(1)}, u32[]{:S(2)}, u32[]{:S(2)}) async-start(bf16[16,64,128]{2,1,0:T(8,128)(2,1)} %bitcast.34), calls=%async_computation.5 | async-start | bytes 524288 | tf_op jit(solution)/shard_map/all_to_all | solution.py:540
  175.8 10.0 %all-to-all-done.5.do_ref = bf16[16,64,128]{2,1,0:T(8,128)(2,1)S(1)} async-done(((bf16[16,64,128]{2,1,0:T(8,128)(2,1)}), bf16[16,64,128]{2,1,0:T(8,128)(2,1)S(1)}, u32[]{:S(2)}, u32[]{:S(2)}) %all-to-all-start.5) | async-done | bytes 262176 | tf_op jit(solution)/shard_map/all_to_all | solution.py:540
  187.0 19.6 %attend_back.1 = (bf16[16,192,128]{2,1,0:T(8,128)(2,1)}, bf16[192,2048]{1,0:T(8,128)(2,1)S(1)}) custom-call(bf16[16,208,128]{2,1,0:T(8,128)(2,1)S(1)} %copy-done.5, bf16[16,64,128]{2,1,0:T(8,128)(2,1)S(1)} %all-to-all-done.5.do_ref, f32[16,64,128]{2,1,0:T(8,128)S(1)} %copy-done.14, f32[8,1,256]{2,1,0:T(1,128)S(1)} %get-tuple-element.33.lse_ref), custom_call_target="tpu_custom_call" | custom-call | flops 1342177280 | bytes 4194304 | tf_op jit(solution)/shard_map/attend_back/pallas_call | solution.py:234
  220.8 21.7 %all-to-all-done.6 = bf16[16,192,128]{2,1,0:T(8,128)(2,1)S(1)} async-done(((bf16[16,192,128]{2,1,0:T(8,128)(2,1)}), bf16[16,192,128]{2,1,0:T(8,128)(2,1)S(1)}, u32[]{:S(2)}, u32[]{:S(2)}) %all-to-all-start.6) | async-done | bytes 786464 | tf_op jit(solution)/shard_map/all_to_all | solution.py:542
  242.4 11.2 %all-to-all-start.8 = ((bf16[8,64,1024]{2,1,0:T(8,128)(2,1)}), bf16[8,64,1024]{2,1,0:T(8,128)(2,1)S(1)}, u32[]{:S(2)}, u32[]{:S(2)}) async-start(bf16[8,64,1024]{2,1,0:T(8,128)(2,1)} %fusion), calls=%async_computation.8 | async-start | bytes 2097152 | tf_op jit(solution)/shard_map/all_to_all | solution.py:559
  254.8 5.9 %fusion.24 = (bf16[1024]{0:T(1024)(128)(2,1)S(1)}, f32[128]{0:T(128)S(1)}, f32[128]{0:T(128)S(1)}, bf16[1024]{0:T(1024)(128)(2,1)S(1)}, f32[128,1024]{1,0:T(8,128)}) fusion(bf16[128,1,1024]{2,0,1:T(8,128)(2,1)S(1)} %copy-done.17, f32[128]{0:T(128)S(1)} %add_rsqrt_fusion.1, f32[128]{0:T(128)S(1)} %broadcast_multiply_fusion.5, f32[1024]{0:T(1024)S(1)} %copy-done.29, ...), kind=kOutput, calls=%fused_computation.53 | convolution fusion | flops 806614784 | bytes 7874560 | tf_op jit(solution)/shard_map/dot_general | solution.py:27
  265.8 13.9 %all-to-all-done.8 = bf16[8,64,1024]{2,1,0:T(8,128)(2,1)S(1)} async-done(((bf16[8,64,1024]{2,1,0:T(8,128)(2,1)}), bf16[8,64,1024]{2,1,0:T(8,128)(2,1)S(1)}, u32[]{:S(2)}, u32[]{:S(2)}) %all-to-all-start.8) | async-done | bytes 1048608 | tf_op jit(solution)/shard_map/all_to_all | solution.py:559
  280.9 4.0 %all-to-all-start.7 = ((bf16[32,112,128]{2,1,0:T(8,128)(2,1)}), bf16[32,112,128]{2,1,0:T(8,128)(2,1)}, u32[]{:S(2)}, u32[]{:S(2)}) async-start(bf16[32,112,128]{2,1,0:T(8,128)(2,1)} %bitcast.43), calls=%async_computation.7 | async-start | bytes 1835008 | tf_op jit(solution)/shard_map/all_to_all | solution.py:619
  295.6 4.4 %collective-permute-done.1 = bf16[64,1024]{1,0:T(8,128)(2,1)S(1)} collective-permute-done((bf16[64,1024]{1,0:T(8,128)(2,1)S(1)}, bf16[64,1024]{1,0:T(8,128)(2,1)S(1)}, u32[]{:S(2)}, u32[]{:S(2)}) %collective-permute-start.1) | collective-permute-done | bytes 131104 | tf_op jit(solution)/shard_map/ppermute | solution.py:405
  300.8 7.4 %all-to-all-done.7 = bf16[32,112,128]{2,1,0:T(8,128)(2,1)} async-done(((bf16[32,112,128]{2,1,0:T(8,128)(2,1)}), bf16[32,112,128]{2,1,0:T(8,128)(2,1)}, u32[]{:S(2)}, u32[]{:S(2)}) %all-to-all-start.7) | async-done | bytes 917536 | tf_op jit(solution)/shard_map/all_to_all | solution.py:619
  329.5 24.2 %slice_grads.1 = (bf16[1024,384]{1,0:T(8,128)(2,1)}, f32[384,1024]{1,0:T(8,128)S(1)}) custom-call(s32[1]{0:T(128)} %bitcast.60.mine_ref, bf16[32,136,1024]{2,1,0:T(8,128)(2,1)S(1)} %bitcast.241, bf16[32,128,1024]{2,1,0:T(8,128)(2,1)S(1)} %bitcast.242, bf16[1024,384]{1,0:T(8,128)(2,1)S(1)} %get-tuple-element.175.up_ref, ...), custom_call_target="tpu_custom_call" | custom-call | flops 12884901888 | bytes 16777216 | tf_op jit(solution)/shard_map/slice_grads/pallas_call | solution.py:353
  353.7 3.9 all-to-all-start.9
  367.5 8.7 %all-to-all-done.9 = bf16[16,64,384]{2,1,0:T(8,128)(2,1)S(1)} async-done(((bf16[16,64,384]{2,1,0:T(8,128)(2,1)}), bf16[16,64,384]{2,1,0:T(8,128)(2,1)S(1)}, u32[]{:S(2)}, u32[]{:S(2)}) %all-to-all-start.9) | async-done | bytes 786464 | tf_op jit(solution)/shard_map/all_to_all | solution.py:582
  380.5 4.3 %collective-permute-done.2 = bf16[16,64,128]{2,1,0:T(8,128)(2,1)S(1)} collective-permute-done((bf16[16,64,128]{2,1,0:T(8,128)(2,1)S(1)}, bf16[16,64,128]{2,1,0:T(8,128)(2,1)S(1)}, u32[]{:S(2)}, u32[]{:S(2)}) %collective-permute-start.2) | collective-permute-done | bytes 262176 | tf_op jit(solution)/shard_map/ppermute | solution.py:405
  (234 shorter events, 117.4 us)
Async XLA Ops:
  7.2 86.3 %copy-start = (bf16[1024,1024]{1,0:T(8,128)(2,1)S(1)}, bf16[1024,1024]{1,0:T(8,128)(2,1)}, u32[]{:S(2)}) copy-start(bf16[1024,1024]{1,0:T(8,128)(2,1)} %param.27) | copy-start | bytes 6291460
  7.2 254.2 %all-gather.6.cloned.1.call-start = ((), (), s32[]{:S(2)}) async-start(), calls=%async_computation.10 | async-start | bytes 4456448 | tf_op jit(solution)/shard_map/all_gather | solution.py:436
  11.6 311.0 %all-gather.10.cloned.1.call-start = ((), (), s32[]{:S(2)}) async-start(), calls=%async_computation.12 | async-start | bytes 8650752 | tf_op jit(solution)/shard_map/all_gather | solution.py:431
  53.1 28.3 %copy-start.32 = (s32[128,1,1]{0,2,1:T(1,128)S(1)}, s32[128,1,1]{0,2,1:T(1,128)}, u32[]{:S(2)}) copy-start(s32[128,1,1]{0,2,1:T(1,128)} %param.21) | copy-start | bytes 1540
  53.1 28.6 %copy-start.37 = (s32[2]{0:T(128)S(1)}, s32[2]{0:T(128)}, u32[]{:S(2)}) copy-start(s32[2]{0:T(128)} %param.22) | copy-start | bytes 28
  53.1 40.4 %copy-start.16 = (bf16[128,1,1024]{2,0,1:T(8,128)(2,1)S(1)}, bf16[128,1,1024]{2,0,1:T(8,128)(2,1)}, u32[]{:S(2)}) copy-start(bf16[128,1,1024]{2,0,1:T(8,128)(2,1)} %param.19) | copy-start | bytes 786436
  71.1 22.4 %all-to-all-start.1 = ((bf16[16,64,128]{2,1,0:T(8,128)(2,1)}), bf16[16,64,128]{2,1,0:T(8,128)(2,1)S(1)}, u32[]{:S(2)}, u32[]{:S(2)}) async-start(bf16[16,64,128]{2,1,0:T(8,128)(2,1)} %get-tuple-element.27), calls=%async_computation.1 | async-start | bytes 524288 | tf_op jit(solution)/shard_map/all_to_all | solution.py:444
  81.3 241.3 %all-gather.8.cloned.1.call-start = ((), (), s32[]{:S(2)}) async-start(), calls=%async_computation.11 | async-start | bytes 9191424 | tf_op jit(solution)/shard_map/all_gather | solution.py:484
  97.8 11.1 %all-to-all-start.2 = ((bf16[2,80,1024]{2,1,0:T(8,128)(2,1)}), bf16[2,80,1024]{2,1,0:T(8,128)(2,1)S(1)}, u32[]{:S(2)}, u32[]{:S(2)}) async-start(bf16[2,80,1024]{2,1,0:T(8,128)(2,1)} %bitcast.255), calls=%async_computation.2 | async-start | bytes 655360 | tf_op jit(solution)/shard_map/all_to_all | solution.py:472
  109.0 9.0 %all-to-all-start.3 = ((bf16[2,80,1024]{2,1,0:T(8,128)(2,1)}), bf16[2,80,1024]{2,1,0:T(8,128)(2,1)S(1)}, u32[]{:S(2)}, u32[]{:S(2)}) async-start(bf16[2,80,1024]{2,1,0:T(8,128)(2,1)} %bitcast.254), calls=%async_computation.3 | async-start | bytes 655360 | tf_op jit(solution)/shard_map/all_to_all | solution.py:472
  139.1 24.4 %all-to-all-start.4 = ((bf16[2,160,1024]{2,1,0:T(8,128)(2,1)}), bf16[2,160,1024]{2,1,0:T(8,128)(2,1)}, u32[]{:S(2)}, u32[]{:S(2)}) async-start(bf16[2,160,1024]{2,1,0:T(8,128)(2,1)} %pad_maximum_fusion.3), calls=%async_computation.4 | async-start | bytes 1310720 | tf_op jit(solution)/shard_map/all_to_all | solution.py:502
  171.2 14.6 %all-to-all-start.5 = ((bf16[16,64,128]{2,1,0:T(8,128)(2,1)}), bf16[16,64,128]{2,1,0:T(8,128)(2,1)S(1)}, u32[]{:S(2)}, u32[]{:S(2)}) async-start(bf16[16,64,128]{2,1,0:T(8,128)(2,1)} %bitcast.34), calls=%async_computation.5 | async-start | bytes 524288 | tf_op jit(solution)/shard_map/all_to_all | solution.py:540
  187.0 24.3 %copy-start.26 = (bf16[16,64,128]{2,1,0:T(8,128)(2,1)S(1)}, bf16[16,64,128]{2,1,0:T(8,128)(2,1)}, u32[]{:S(2)}) copy-start(bf16[16,64,128]{2,1,0:T(8,128)(2,1)} %copy-done.25) | copy-start | bytes 786436
  207.4 35.0 %all-to-all-start.6 = ((bf16[16,192,128]{2,1,0:T(8,128)(2,1)}), bf16[16,192,128]{2,1,0:T(8,128)(2,1)S(1)}, u32[]{:S(2)}, u32[]{:S(2)}) async-start(bf16[16,192,128]{2,1,0:T(8,128)(2,1)} %get-tuple-element.34), calls=%async_computation.6 | async-start | bytes 1572864 | tf_op jit(solution)/shard_map/all_to_all | solution.py:542
  215.1 2.7 collective-permute-start
  220.8 33.8 %copy-start.36 = (f32[2]{0:T(128)S(1)}, f32[2]{0:T(128)}, u32[]{:S(2)}) copy-start(f32[2]{0:T(128)} %get-tuple-element.117) | copy-start | bytes 28
  220.8 34.0 %copy-start.17 = (bf16[128,1,1024]{2,0,1:T(8,128)(2,1)S(1)}, bf16[128,1,1024]{2,0,1:T(8,128)(2,1)}, u32[]{:S(2)}) copy-start(bf16[128,1,1024]{2,0,1:T(8,128)(2,1)} %param.19) | copy-start | bytes 786436
  220.8 34.0 %copy-start.29 = (f32[1024]{0:T(1024)S(1)}, f32[1024]{0:T(1024)}, u32[]{:S(2)}) copy-start(f32[1024]{0:T(1024)} %param.24) | copy-start | bytes 12292
  242.4 37.3 %all-to-all-start.8 = ((bf16[8,64,1024]{2,1,0:T(8,128)(2,1)}), bf16[8,64,1024]{2,1,0:T(8,128)(2,1)S(1)}, u32[]{:S(2)}, u32[]{:S(2)}) async-start(bf16[8,64,1024]{2,1,0:T(8,128)(2,1)} %fusion), calls=%async_computation.8 | async-start | bytes 2097152 | tf_op jit(solution)/shard_map/all_to_all | solution.py:559
  280.9 27.4 %all-to-all-start.7 = ((bf16[32,112,128]{2,1,0:T(8,128)(2,1)}), bf16[32,112,128]{2,1,0:T(8,128)(2,1)}, u32[]{:S(2)}, u32[]{:S(2)}) async-start(bf16[32,112,128]{2,1,0:T(8,128)(2,1)} %bitcast.43), calls=%async_computation.7 | async-start | bytes 1835008 | tf_op jit(solution)/shard_map/all_to_all | solution.py:619
  292.9 7.2 %collective-permute-start.1 = (bf16[64,1024]{1,0:T(8,128)(2,1)S(1)}, bf16[64,1024]{1,0:T(8,128)(2,1)S(1)}, u32[]{:S(2)}, u32[]{:S(2)}) collective-permute-start(bf16[64,1024]{1,0:T(8,128)(2,1)S(1)} %reduce_sum.304), channel_id=1, source_target_pairs={{0,1},{1,0},{2,3},{3,2},{4,5},{5,4},{6,7},{7,6},{8,9},{9,8},{10,11... | collective-permute-start | bytes 393224 | tf_op jit(solution)/shard_map/ppermute | solution.py:405
  353.7 22.5 %all-to-all-start.9 = ((bf16[16,64,384]{2,1,0:T(8,128)(2,1)}), bf16[16,64,384]{2,1,0:T(8,128)(2,1)S(1)}, u32[]{:S(2)}, u32[]{:S(2)}) async-start(bf16[16,64,384]{2,1,0:T(8,128)(2,1)} %bitcast.72), calls=%async_computation.9 | async-start | bytes 1572864 | tf_op jit(solution)/shard_map/all_to_all | solution.py:582
  357.6 8.6 %collective-permute-start.3 = (bf16[128,1024]{1,0:T(8,128)(2,1)S(1)}, bf16[128,1024]{1,0:T(8,128)(2,1)S(1)}, u32[]{:S(2)}, u32[]{:S(2)}) collective-permute-start(bf16[128,1024]{1,0:T(8,128)(2,1)S(1)} %slice.175), channel_id=1, source_target_pairs={{0,1},{1,0},{2,3},{3,2},{4,5},{5,4},{6,7},{7,6},{8,9},{9,8},{10,11... | collective-permute-start | bytes 786440 | tf_op jit(solution)/shard_map/ppermute | solution.py:405
  376.3 8.5 %collective-permute-start.2 = (bf16[16,64,128]{2,1,0:T(8,128)(2,1)S(1)}, bf16[16,64,128]{2,1,0:T(8,128)(2,1)S(1)}, u32[]{:S(2)}, u32[]{:S(2)}) collective-permute-start(bf16[16,64,128]{2,1,0:T(8,128)(2,1)S(1)} %slice.133), channel_id=1, source_target_pairs={{0,1},{1,0},{2,3},{3,2},{4,5},{5,4},{6,7},{7,6},{8,9},{9,8},{10,11... | collective-permute-start | bytes 786440 | tf_op jit(solution)/shard_map/ppermute | solution.py:405
  (33 other events, 142.5 us)
Sparse Core Ops, SparseCore 0:
  11.7 61.4 all-gather.5
  76.2 80.2 all-gather.9
  159.4 94.5 all-gather.7
